TPU v7x, 32 devices: a whole 2x2x4 slice. The times are simulated.
32 devices in a mesh: ctx: 8 (over z, core), rep: 4 (over y, x).
Axes of the slice: x: 2, y: 2, z: 4, core: 2. Of those that a mesh axis runs over, the one named last changes fastest.
Arguments:
- queries: bfloat16 [512, 8192], P(None, 'ctx'), may hold values from -6 to 6
- keys: bfloat16 [4096, 1024], P(('ctx', 'rep')), may hold values from -6 to 6
- values: bfloat16 [4096, 1024], P(('ctx', 'rep')), may hold values from -6 to 6
- forward_output: bfloat16 [512, 8192], P(None, 'ctx'), may hold values from -6 to 6
- output_gradient: bfloat16 [512, 8192], P(None, 'ctx'), may hold values from -6 to 6
- log_sum_norm: float32 [64, 512], P('ctx'), may hold values from 3 to 5
- block_attend_mask: int32 [64, 4, 32], P('ctx'), may hold values from 0 to 1, as said below
Outputs:
- grad_queries: bfloat16 [512, 8192], P('rep', 'ctx')
- key_gradient: bfloat16 [4096, 1024], P(('ctx', 'rep'))
- value_gradient: bfloat16 [4096, 1024], P(('ctx', 'rep'))
Inputs may be any that keep to these rules, and one draw needn't show every extreme that they name: `block_attend_mask`: 1 where a query block of a query head attends a key block of 128 tokens, else 0; how many key blocks are attended differs from head to head.
All inputs are finite; a program needn't handle non-finite values.
Results may differ from a plain program's by a relative error of at most 0.007.
Values may be sent and summed in bfloat16 or wider, within the bound.
A program may use at most 64 MiB of HBM per device.

v0:
```python
import jax
import jax.numpy as jnp
from jax import lax
from jax.sharding import PartitionSpec as P

KEY_VALUE_HEADS = 8
HEAD_SIZE = 128
BLK = 128
SLAB_QUERIES = 512


def on_device(
    queries, keys, values, forward_output, output_gradient, log_sum_norm, block_attend_mask
):
    context_length = lax.axis_size("ctx")
    rep_size = lax.axis_size("rep")
    group_width = context_length // KEY_VALUE_HEADS
    heads_dev = queries.shape[1] // HEAD_SIZE
    keys_local_share = keys.shape[0]
    span_len = context_length * keys_local_share
    block_count = span_len // BLK
    query_block_count = SLAB_QUERIES // BLK
    softmax_scale = HEAD_SIZE ** (-0.5)
    rep_pos = lax.axis_index("rep")
    bit_total = group_width.bit_length() - 1

    def spread(number_array):
        widened = jnp.broadcast_to(
            number_array.reshape(keys_local_share, KEY_VALUE_HEADS, 1, HEAD_SIZE),
            (keys_local_share, KEY_VALUE_HEADS, group_width, HEAD_SIZE),
        )
        return widened.reshape(keys_local_share, context_length, HEAD_SIZE)

    arrived_keys, arrived_values = (
        lax.all_to_all(spread(keys), "ctx", split_axis=1, concat_axis=0, tiled=True),
        lax.all_to_all(spread(values), "ctx", split_axis=1, concat_axis=0, tiled=True),
    )
    key_span = arrived_keys.reshape(span_len, HEAD_SIZE)
    value_span = arrived_values.reshape(span_len, HEAD_SIZE)
    query_heads = queries.reshape(SLAB_QUERIES, heads_dev, HEAD_SIZE).transpose(1, 0, 2)
    cotan_heads = output_gradient.reshape(SLAB_QUERIES, heads_dev, HEAD_SIZE).transpose(1, 0, 2)
    row_dots = jnp.sum(
        (output_gradient.astype(jnp.float32) * forward_output.astype(jnp.float32)).reshape(
            SLAB_QUERIES, heads_dev, HEAD_SIZE
        ),
        axis=2,
    ).T
    mask_local = block_attend_mask.reshape(
        heads_dev, query_block_count, context_length, rep_size, keys_local_share // BLK
    )
    mask_span = lax.dynamic_index_in_dim(mask_local, rep_pos, 3, keepdims=False).reshape(
        heads_dev, query_block_count, block_count
    )
    tile_count = 4
    key_blocks = key_span.reshape(block_count, BLK, HEAD_SIZE)
    value_blocks = value_span.reshape(block_count, BLK, HEAD_SIZE)
    start_totals = (
        jnp.zeros((block_count, BLK, HEAD_SIZE), jnp.float32),
        jnp.zeros((block_count, BLK, HEAD_SIZE), jnp.float32),
        jnp.zeros((heads_dev, SLAB_QUERIES, HEAD_SIZE), jnp.float32),
    )
    used_blocks = jnp.max(mask_span, axis=(0, 1))
    block_order = jnp.argsort(1 - used_blocks, stable=True)
    live_count = jnp.sum(used_blocks)
    turn_total = (live_count + tile_count - 1) // tile_count

    def one_turn(turn, carry):
        key_total, value_total, query_total = carry
        picked = lax.dynamic_slice_in_dim(block_order, turn * tile_count, tile_count)
        live_flags = (
            turn * tile_count + jnp.arange(tile_count, dtype=jnp.int32) < live_count
        ).astype(jnp.int32)
        key_tile = jnp.take(key_blocks, picked, axis=0).reshape(tile_count * BLK, HEAD_SIZE)
        value_tile = jnp.take(value_blocks, picked, axis=0).reshape(tile_count * BLK, HEAD_SIZE)
        mask_tile = jnp.take(mask_span, picked, axis=2) * live_flags[None, None, :]
        mask_full = jnp.broadcast_to(
            mask_tile[:, :, None, :, None].astype(jnp.float32),
            (heads_dev, query_block_count, BLK, tile_count, BLK),
        ).reshape(heads_dev, SLAB_QUERIES, tile_count * BLK)
        scores = (
            jnp.einsum("hqd,kd->hqk", query_heads, key_tile, preferred_element_type=jnp.float32)
            * softmax_scale
        )
        weights_f = jnp.exp(scores - log_sum_norm[:, :, None]) * mask_full
        weights_b = weights_f.astype(jnp.bfloat16)
        grad_weights = jnp.einsum(
            "hqd,kd->hqk", cotan_heads, value_tile, preferred_element_type=jnp.float32
        )
        grad_scores = (weights_f * (grad_weights - row_dots[:, :, None])).astype(jnp.bfloat16)
        value_part = jnp.einsum(
            "hqk,hqd->kd", weights_b, cotan_heads, preferred_element_type=jnp.float32
        ).reshape(tile_count, BLK, HEAD_SIZE)
        key_part = jnp.einsum(
            "hqk,hqd->kd", grad_scores, query_heads, preferred_element_type=jnp.float32
        ).reshape(tile_count, BLK, HEAD_SIZE)
        query_total = query_total + jnp.einsum(
            "hqk,kd->hqd", grad_scores, key_tile, preferred_element_type=jnp.float32
        )
        key_total = key_total.at[picked].add(key_part)
        value_total = value_total.at[picked].add(value_part)
        return (key_total, value_total, query_total)

    key_total, value_total, query_total = lax.fori_loop(0, turn_total, one_turn, start_totals)
    key_scaled = key_total * softmax_scale
    query_terms = (
        (query_total * softmax_scale)
        .transpose(1, 0, 2)
        .reshape(SLAB_QUERIES, heads_dev * HEAD_SIZE)
    )
    grad_queries = lax.psum_scatter(query_terms, "rep", scatter_dimension=0, tiled=True).astype(
        jnp.bfloat16
    )
    grad_parts = jnp.stack([key_scaled, value_total]).astype(jnp.bfloat16)
    returned_value = lax.all_to_all(grad_parts, "ctx", split_axis=1, concat_axis=1, tiled=True)
    level_width = group_width
    joined_result = returned_value.reshape(
        2, KEY_VALUE_HEADS, group_width, keys_local_share, HEAD_SIZE
    )
    for bit_number in range(bit_total):
        level_width = level_width // 2
        paired_items = joined_result.reshape(
            2, KEY_VALUE_HEADS, level_width, 2, keys_local_share, HEAD_SIZE
        ).astype(jnp.float32)
        joined_result = (paired_items[:, :, :, 0] + paired_items[:, :, :, 1]).astype(jnp.bfloat16)
    joined_result = joined_result.reshape(2, KEY_VALUE_HEADS, keys_local_share, HEAD_SIZE)
    closing_gradients = jnp.transpose(joined_result, (0, 2, 1, 3)).reshape(
        2, keys_local_share, KEY_VALUE_HEADS * HEAD_SIZE
    )
    return (grad_queries, closing_gradients[0], closing_gradients[1])


def solution(mesh):
    in_specs = (
        P(None, "ctx"),
        P(("ctx", "rep"), None),
        P(("ctx", "rep"), None),
        P(None, "ctx"),
        P(None, "ctx"),
        P("ctx", None),
        P("ctx", None, None),
    )
    out_specs = (P("rep", "ctx"), P(("ctx", "rep"), None), P(("ctx", "rep"), None))
    return jax.shard_map(
        on_device, mesh=mesh, in_specs=in_specs, out_specs=out_specs, check_vma=False
    )
```

profile of v0, /device:TPU:0, one launch (start us, length us, event | category | flops | bytes accessed | tf_op | source)
XLA Modules:
  0.0 166.4 jit_solution(2927434936848976536)
XLA Ops:
  7.2 1.9 %copy.64 = bf16[128,1024]{0,1:T(8,128)(2,1)} copy(bf16[128,1024]{1,0:T(8,128)(2,1)} %param.12) | data formatting | bytes 524288 | tf_op args[1]
  9.1 6.3 %all-to-all-start = ((bf16[128,8,128]{0,2,1:T(8,128)(2,1)}), bf16[128,8,128]{0,2,1:T(8,128)(2,1)S(1)}, u32[]{:S(2)}, u32[]{:S(2)}) async-start(bf16[128,8,128]{0,2,1:T(8,128)(2,1)} %bitcast.13), calls=%async_computation | async-start | bytes 524288 | tf_op jit(solution)/shard_map/all_to_all | solution.py:35
  16.2 1.8 %copy.67 = bf16[128,1024]{0,1:T(8,128)(2,1)} copy(bf16[128,1024]{1,0:T(8,128)(2,1)} %param.13) | data formatting | bytes 524288 | tf_op args[2]
  18.2 6.9 %all-to-all-done = bf16[128,8,128]{0,2,1:T(8,128)(2,1)S(1)} async-done(((bf16[128,8,128]{0,2,1:T(8,128)(2,1)}), bf16[128,8,128]{0,2,1:T(8,128)(2,1)S(1)}, u32[]{:S(2)}, u32[]{:S(2)}) %all-to-all-start) | async-done | bytes 262176 | tf_op jit(solution)/shard_map/all_to_all | solution.py:35
  25.1 4.0 %all-to-all-start.1 = ((bf16[128,8,128]{0,2,1:T(8,128)(2,1)}), bf16[128,8,128]{0,2,1:T(8,128)(2,1)}, u32[]{:S(2)}, u32[]{:S(2)}) async-start(bf16[128,8,128]{0,2,1:T(8,128)(2,1)} %bitcast.20), calls=%async_computation.1 | async-start | bytes 524288 | tf_op jit(solution)/shard_map/all_to_all | solution.py:36
  32.1 1.6 multiply_bitcast_fusion.1
  39.7 1.8 %copy.72 = bf16[8,128,128]{2,1,0:T(8,128)(2,1)} copy(bf16[8,128,128]{1,2,0:T(8,128)(2,1)} %bitcast.23) | data formatting | bytes 524288 | tf_op jit(solution)/shard_map/while | solution.py:103
  43.1 74.7 %while.14 = (s32[]{:T(128)}, f32[8,128,128]{2,1,0:T(8,128)S(1)}, f32[8,128,128]{2,1,0:T(8,128)S(1)}, f32[8,512,128]{2,1,0:T(8,128)}, s32[]{:T(128)}, /*index=5*/...) while((s32[]{:T(128)}, f32[8,128,128]{2,1,0:T(8,128)S(1)}, ...), condition=%wide.region_7.9_spmd, body=%wide.region_4.8_spmd.sunk | while | flops 2699822592 | bytes 133603296 | solution.py:103
  44.7 4.4 %broadcast_in_dim.52 = f32[8,4,128,4,128]{2,1,4,3,0:T(4,128)} broadcast(f32[8,4,4]{1,2,0:T(4,128)S(1)} %copy.86), dimensions={0,1,3} | broadcast | bytes 8389120 | tf_op jit(solution)/shard_map/while/body/broadcast_in_dim | solution.py:76
  49.1 10.3 %reshape.151 = f32[8,512,512]{1,2,0:T(8,128)} reshape(f32[8,4,128,4,128]{2,1,4,3,0:T(4,128)} %broadcast_in_dim.52) | data formatting | bytes 16777216 | tf_op jit(solution)/shard_map/while/body/reshape | solution.py:79
  62.6 5.2 %bitcast_multiply_fusion.3 = f32[8,512,512]{1,2,0:T(8,128)S(1)} fusion(f32[8,512,512]{1,2,0:T(8,128)} %reshape.151, f32[8,512]{1,0:T(8,128)S(1)} %get-tuple-element.324, bf16[512,128,1]{1,0,2:T(8,128)(2,1)S(1)} %bitcast.101, bf16[8,512,128]{2,1,0:T(8,128)(2,1)S(1)} %get-tuple-element.323), kind=kOutput, calls=%fused_computation.7.clone.1 | convolution fusion | flops 543162368 | bytes 17973248 | tf_op jit(solution)/shard_map/while/body/hqd,kd->hqk/dot_general | solution.py:81
  69.1 2.2 %copy-done = f32[8,512,512]{1,2,0:T(8,128)} copy-done((f32[8,512,512]{1,2,0:T(8,128)}, f32[8,512,512]{1,2,0:T(8,128)S(1)}, u32[]{:S(2)}) %copy-start) | copy-done | bytes 8388632 | tf_op jit(solution)/shard_map/while
  71.4 1.7 %convolution_add_fusion.2 = f32[8,512,128]{2,1,0:T(8,128)S(1)} fusion(f32[8,512,128]{2,1,0:T(8,128)S(1)} %copy-done.1, bf16[8,512,512]{1,2,0:T(8,128)(2,1)S(1)} %fusion.39, bf16[512,128,1]{1,0,2:T(8,128)(2,1)S(1)} %bitcast.102), kind=kOutput, calls=%fused_computation.10.clone.1 | convolution fusion | flops 537395200 | bytes 8519680 | tf_op jit(solution)/shard_map/while/body/hqk,kd->hqd/dot_general | solution.py:96
  75.1 4.6 %fusion.41 = f32[512,128,1]{1,0,2:T(8,128)S(1)} fusion(bf16[8,512,128]{2,1,0:T(8,128)(2,1)S(1)} %get-tuple-element.328, f32[8,512,512]{1,2,0:T(8,128)} %copy-done), kind=kOutput, calls=%fused_computation.8.clone.1 | convolution fusion | flops 538968064 | bytes 9699328 | tf_op jit(solution)/shard_map/while/body/hqk,hqd->kd/dot_general | solution.py:90
  82.0 4.4 %broadcast_in_dim.52 = f32[8,4,128,4,128]{2,1,4,3,0:T(4,128)} broadcast(f32[8,4,4]{1,2,0:T(4,128)S(1)} %copy.86), dimensions={0,1,3} | broadcast | bytes 8389120 | tf_op jit(solution)/shard_map/while/body/broadcast_in_dim | solution.py:76
  86.4 10.3 %reshape.151 = f32[8,512,512]{1,2,0:T(8,128)} reshape(f32[8,4,128,4,128]{2,1,4,3,0:T(4,128)} %broadcast_in_dim.52) | data formatting | bytes 16777216 | tf_op jit(solution)/shard_map/while/body/reshape | solution.py:79
  99.8 5.2 %bitcast_multiply_fusion.3 = f32[8,512,512]{1,2,0:T(8,128)S(1)} fusion(f32[8,512,512]{1,2,0:T(8,128)} %reshape.151, f32[8,512]{1,0:T(8,128)S(1)} %get-tuple-element.324, bf16[512,128,1]{1,0,2:T(8,128)(2,1)S(1)} %bitcast.101, bf16[8,512,128]{2,1,0:T(8,128)(2,1)S(1)} %get-tuple-element.323), kind=kOutput, calls=%fused_computation.7.clone.1 | convolution fusion | flops 543162368 | bytes 17973248 | tf_op jit(solution)/shard_map/while/body/hqd,kd->hqk/dot_general | solution.py:81
  106.4 2.2 %copy-done = f32[8,512,512]{1,2,0:T(8,128)} copy-done((f32[8,512,512]{1,2,0:T(8,128)}, f32[8,512,512]{1,2,0:T(8,128)S(1)}, u32[]{:S(2)}) %copy-start) | copy-done | bytes 8388632 | tf_op jit(solution)/shard_map/while
  108.6 1.7 convolution_add_fusion.2
  112.4 4.6 %fusion.41 = f32[512,128,1]{1,0,2:T(8,128)S(1)} fusion(bf16[8,512,128]{2,1,0:T(8,128)(2,1)S(1)} %get-tuple-element.328, f32[8,512,512]{1,2,0:T(8,128)} %copy-done), kind=kOutput, calls=%fused_computation.8.clone.1 | convolution fusion | flops 538968064 | bytes 9699328 | tf_op jit(solution)/shard_map/while/body/hqk,hqd->kd/dot_general | solution.py:90
  117.8 3.2 %copy_bitcast_fusion = f32[512,1024]{1,0:T(8,128)} fusion(f32[8,512,128]{2,1,0:T(8,128)} %get-tuple-element.81), kind=kLoop, calls=%fused_computation.18 | loop fusion | flops 524288 | bytes 4194304 | tf_op jit(solution)/shard_map/reshape | solution.py:108
  121.3 20.1 %all_to_all.35 = bf16[2,8,128,128]{3,2,0,1:T(8,128)(2,1)S(1)} all-to-all(bf16[2,8,128,128]{3,2,0,1:T(8,128)(2,1)S(1)} %pad_maximum_fusion), channel_id=1, replica_groups=mesh['ctx'=8,'rep'=4] {'ctx'}, dimensions={1} | all-to-all | bytes 1048576 | tf_op jit(solution)/shard_map/all_to_all | solution.py:114
  143.4 14.3 %reduce-scatter.2.cloned.1.call-done = f32[128,1024]{1,0:T(8,128)} async-done(((f32[512,1024]{1,0:T(8,128)}), f32[128,1024]{1,0:T(8,128)}) %reduce-scatter.2.cloned.1.call-update) | async-done | bytes 524304 | tf_op jit(solution)/shard_map/reduce_scatter | solution.py:110
  157.8 1.8 %convert_element_type.33 = bf16[128,1024]{1,0:T(8,128)(2,1)} convert(f32[128,1024]{1,0:T(8,128)} %reduce-scatter.2.cloned.1.call-done) | non-fusion elementwise | flops 131072 | bytes 786432 | tf_op jit(solution)/shard_map/convert_element_type | solution.py:110
  (68 shorter events, 30.4 us)
Async XLA Ops:
  7.2 24.9 %copy-start.3 = (bf16[512,1024]{1,0:T(8,128)(2,1)S(1)}, bf16[512,1024]{1,0:T(8,128)(2,1)}, u32[]{:S(2)}) copy-start(bf16[512,1024]{1,0:T(8,128)(2,1)} %param.15) | copy-start | bytes 3145732
  9.1 16.1 %all-to-all-start = ((bf16[128,8,128]{0,2,1:T(8,128)(2,1)}), bf16[128,8,128]{0,2,1:T(8,128)(2,1)S(1)}, u32[]{:S(2)}, u32[]{:S(2)}) async-start(bf16[128,8,128]{0,2,1:T(8,128)(2,1)} %bitcast.13), calls=%async_computation | async-start | bytes 524288 | tf_op jit(solution)/shard_map/all_to_all | solution.py:35
  25.1 6.9 %copy-start.4 = (bf16[128,8,128]{0,2,1:T(8,128)(2,1)}, bf16[128,8,128]{0,2,1:T(8,128)(2,1)S(1)}, u32[]{:S(2)}) copy-start(bf16[128,8,128]{0,2,1:T(8,128)(2,1)S(1)} %all-to-all-done) | copy-start | bytes 786436
  25.1 14.6 %all-to-all-start.1 = ((bf16[128,8,128]{0,2,1:T(8,128)(2,1)}), bf16[128,8,128]{0,2,1:T(8,128)(2,1)}, u32[]{:S(2)}, u32[]{:S(2)}) async-start(bf16[128,8,128]{0,2,1:T(8,128)(2,1)} %bitcast.20), calls=%async_computation.1 | async-start | bytes 524288 | tf_op jit(solution)/shard_map/all_to_all | solution.py:36
  29.2 128.6 %reduce-scatter.2.cloned.1.call-start = ((), (), s32[]{:S(2)}) async-start(), calls=%async_computation.4 | async-start | bytes 2621440 | tf_op jit(solution)/shard_map/reduce_scatter | solution.py:110
  34.9 4.0 %copy-start.5 = (bf16[128,8,128]{0,2,1:T(8,128)(2,1)S(1)}, bf16[128,8,128]{0,2,1:T(8,128)(2,1)}, u32[]{:S(2)}) copy-start(bf16[128,8,128]{0,2,1:T(8,128)(2,1)} %copy-done.4) | copy-start | bytes 786436
  36.4 6.7 %copy-start.6 = (f32[8,512]{1,0:T(8,128)S(1)}, f32[8,512]{1,0:T(8,128)}, u32[]{:S(2)}) copy-start(f32[8,512]{1,0:T(8,128)} %param.16) | copy-start | bytes 49156
  67.8 3.5 %copy-start = (f32[8,512,512]{1,2,0:T(8,128)}, f32[8,512,512]{1,2,0:T(8,128)S(1)}, u32[]{:S(2)}) copy-start(f32[8,512,512]{1,2,0:T(8,128)S(1)} %bitcast_multiply_fusion.3) | copy-start | bytes 25165828 | tf_op jit(solution)/shard_map/while
  67.8 3.5 %copy-start.1 = (f32[8,512,128]{2,1,0:T(8,128)S(1)}, f32[8,512,128]{2,1,0:T(8,128)}, u32[]{:S(2)}) copy-start(f32[8,512,128]{2,1,0:T(8,128)} %get-tuple-element.301) | copy-start | bytes 6291460 | tf_op jit(solution)/shard_map/while
  73.0 1.4 copy-start.2
  105.1 3.5 %copy-start = (f32[8,512,512]{1,2,0:T(8,128)}, f32[8,512,512]{1,2,0:T(8,128)S(1)}, u32[]{:S(2)}) copy-start(f32[8,512,512]{1,2,0:T(8,128)S(1)} %bitcast_multiply_fusion.3) | copy-start | bytes 25165828 | tf_op jit(solution)/shard_map/while
  105.1 3.5 %copy-start.1 = (f32[8,512,128]{2,1,0:T(8,128)S(1)}, f32[8,512,128]{2,1,0:T(8,128)}, u32[]{:S(2)}) copy-start(f32[8,512,128]{2,1,0:T(8,128)} %get-tuple-element.301) | copy-start | bytes 6291460 | tf_op jit(solution)/shard_map/while
  110.3 1.4 copy-start.2
Sparse Core Ops, SparseCore 0:
  121.2 36.5 reduce-scatter.1
where the time goes:
time: 168 us; the launch traced here: 166 us
  local copies, waits for them, and re-layouts  57.1 us (34%)
  matrix products  28.1 us (17%)
  waiting for transfers between devices  21.3 us (13%)
  blocking collectives  20.1 us (12%)
  between operations  14.8 us (9%)
  other arithmetic  14.1 us (8%)
  starting transfers between devices  10.4 us (6%)
    reshape x2, local copies, waits for them, and re-layouts, one_turn(): mask_full = jnp.broadcast_to(mask_tile[:, :, None, :, None].astype(jnp.fl...  20.6 us
    all_to_all x1, blocking collectives, on_device(): lax.all_to_all(grad_parts, 'ctx', split_axis=1, concat_axis=1, tiled=True)  20.1 us
    reduce_scatter x1, waiting for transfers between devices, on_device(): lax.psum_scatter(query_terms, 'rep', scatter_dimension=0, tiled=True)  14.3 us
    dot_general x2, matrix products, one_turn(): jnp.einsum('hqd,kd->hqk', query_heads, key_tile, preferred_element_type=j...  10.5 us
    unnamed x16, local copies, waits for them, and re-layouts  9.7 us
    dot_general x2, matrix products, one_turn(): jnp.einsum('hqk,hqd->kd', weights_b, cotan_heads, preferred_element_type=...  9.25 us
    broadcast_in_dim x2, local copies, waits for them, and re-layouts, one_turn(): jnp.broadcast_to(mask_tile[:, :, None, :, None].astype(jnp.float32), (hea...  8.75 us
    all_to_all x1, waiting for transfers between devices, on_device(): lax.all_to_all(spread(keys), 'ctx', split_axis=1, concat_axis=0, tiled=True)  6.91 us
  transfers between devices with their start and end apart: 3, of which 2 were waited for; matrix products, arithmetic and copies ran while one was open for 9% of the time, Pallas kernels for 0%

commit v1 on v0

v1 whole, which is shorter than its diff:
```python
import functools

import jax
import jax.numpy as jnp
from jax import lax
from jax.experimental import pallas as pl
from jax.experimental.pallas import tpu as pltpu
from jax.sharding import PartitionSpec as P

KEY_VALUE_HEADS = 8
HEAD_SIZE = 128
BLK = 128
MESH = pl.DeviceIdType.MESH
LOG2_E = 1.4426950408889634
MASKED = 1e30


def partner_of(index, step, count):
    total = 0
    bit = 1
    while bit < count:
        total = total + ((index // bit + step // bit) % 2) * bit
        bit *= 2
    return total


def kernel(
    n_ctx,
    n_rep,
    heads,
    group,
    keys,
    values,
    queries,
    fwd_out,
    grad_out,
    norm,
    mask,
    dq_out,
    dkv_out,
    q_v,
    o_v,
    g_v,
    qt_v,
    gt_v,
    norm_b,
    dots_b,
    kv_v,
    dk_acc,
    dv_acc,
    dq_acc,
    dkv_send,
    dq_send,
    dq_land,
    dkv_land,
    load_sem,
    kv_send_sem,
    kv_recv_sem,
    d_send_sem,
    d_recv_sem,
    q_send_sem,
    q_recv_sem,
):
    ctx = lax.axis_index("ctx")
    rep = lax.axis_index("rep")
    n_q = q_v.shape[0]
    rows = n_q // n_rep
    scale = HEAD_SIZE ** (-0.5)

    def head_cols(head):
        return pl.ds(pl.multiple_of(head * HEAD_SIZE, HEAD_SIZE), HEAD_SIZE)

    my_head = ctx // group
    my_cols = head_cols(my_head)

    loads = [
        pltpu.make_async_copy(keys.at[:, my_cols], kv_v.at[ctx, 0], load_sem.at[0]),
        pltpu.make_async_copy(values.at[:, my_cols], kv_v.at[ctx, 1], load_sem.at[1]),
        pltpu.make_async_copy(grad_out, g_v, load_sem.at[2]),
        pltpu.make_async_copy(fwd_out, o_v, load_sem.at[3]),
        pltpu.make_async_copy(queries, q_v, load_sem.at[4]),
    ]
    for load in loads:
        load.start()

    barrier = pltpu.get_barrier_semaphore()

    @pl.loop(1, n_ctx)
    def _(step):
        peer = partner_of(ctx, step, n_ctx)
        pl.semaphore_signal(barrier, inc=1, device_id=(peer, rep), device_id_type=MESH)

    @pl.loop(1, n_rep)
    def _(step):
        peer = partner_of(rep, step, n_rep)
        pl.semaphore_signal(barrier, inc=1, device_id=(ctx, peer), device_id_type=MESH)

    pl.semaphore_wait(barrier, n_ctx - 1 + n_rep - 1)

    def kv_copy(step, kind):
        peer = partner_of(ctx, step, n_ctx)
        source = (keys, values)[kind]
        return pltpu.make_async_remote_copy(
            src_ref=source.at[:, head_cols(peer // group)],
            dst_ref=kv_v.at[ctx, kind],
            send_sem=kv_send_sem.at[step, kind],
            recv_sem=kv_recv_sem.at[step, kind],
            device_id=(peer, rep),
            device_id_type=MESH,
        )

    def kv_arrival(step, kind):
        peer = partner_of(ctx, step, n_ctx)
        return pltpu.make_async_remote_copy(
            src_ref=(keys, values)[kind].at[:, my_cols],
            dst_ref=kv_v.at[peer, kind],
            send_sem=kv_send_sem.at[step, kind],
            recv_sem=kv_recv_sem.at[step, kind],
            device_id=(peer, rep),
            device_id_type=MESH,
        )

    @pl.loop(1, n_ctx)
    def _(step):
        kv_copy(step, 0).start()
        kv_copy(step, 1).start()

    for load in loads:
        load.wait()

    @pl.loop(0, heads)
    def _(head):
        cols = head_cols(head)
        g = g_v[:, cols]
        q = q_v[:, cols]
        dots = jnp.sum(g.astype(jnp.float32) * o_v[:, cols].astype(jnp.float32), axis=1, keepdims=True)
        dots_b[head] = jnp.broadcast_to(dots, (n_q, BLK))
        row = norm[pl.ds(head, 1), :] * LOG2_E
        norm_b[head] = jnp.broadcast_to(row, (BLK, n_q)).T
        qt_v[head] = q.T
        gt_v[head] = g.T
        dq_acc[head] = jnp.zeros((n_q, HEAD_SIZE), jnp.float32)

    def landing(source, kind):
        place = head_cols(source // group)
        if group == 1:
            return dkv_out.at[kind, :, place]
        return dkv_land.at[source % group, kind, :, place]

    def d_copy(step, kind):
        peer = partner_of(ctx, step, n_ctx)
        return pltpu.make_async_remote_copy(
            src_ref=dkv_send.at[step, kind],
            dst_ref=landing(ctx, kind),
            send_sem=d_send_sem.at[step, kind],
            recv_sem=d_recv_sem.at[step, kind],
            device_id=(peer, rep),
            device_id_type=MESH,
        )

    def d_arrival(step, kind):
        peer = partner_of(ctx, step, n_ctx)
        return pltpu.make_async_remote_copy(
            src_ref=dkv_send.at[step, kind],
            dst_ref=landing(peer, kind),
            send_sem=d_send_sem.at[step, kind],
            recv_sem=d_recv_sem.at[step, kind],
            device_id=(peer, rep),
            device_id_type=MESH,
        )

    def q_copy(step, head):
        peer = partner_of(rep, step, n_rep)
        at = pl.ds(pl.multiple_of(peer * rows, rows), rows)
        return pltpu.make_async_remote_copy(
            src_ref=dq_send.at[head, at],
            dst_ref=dq_land.at[step, head],
            send_sem=q_send_sem.at[step, head],
            recv_sem=q_recv_sem.at[step, head],
            device_id=(ctx, peer),
            device_id_type=MESH,
        )

    def compute(step, head):
        source = partner_of(ctx, step, n_ctx)
        cols = head_cols(head)
        k = kv_v[source, 0]
        v = kv_v[source, 1]
        q = q_v[:, cols]
        g = g_v[:, cols]
        nt = (((1,), (1,)), ((), ()))
        s = lax.dot_general(q, k, nt, preferred_element_type=jnp.float32)
        gw = lax.dot_general(g, v, nt, preferred_element_type=jnp.float32)
        key_block = source * n_rep + rep
        parts = []
        for qb in range(n_q // BLK):
            off = (1 - mask[head, qb, key_block]).astype(jnp.float32) * MASKED
            span = slice(qb * BLK, (qb + 1) * BLK)
            parts.append(jnp.exp2(s[span] * (scale * LOG2_E) - (norm_b[head, span, :] + off)))
        w = jnp.concatenate(parts, axis=0)
        p = w.astype(jnp.bfloat16)
        ds = (w * (gw - dots_b[head])).astype(jnp.bfloat16)
        dk_acc[...] += jnp.dot(qt_v[head], ds, preferred_element_type=jnp.float32)
        dv_acc[...] += jnp.dot(gt_v[head], p, preferred_element_type=jnp.float32)
        return dq_acc[head] + jnp.dot(ds, k, preferred_element_type=jnp.float32)

    def clear():
        dk_acc[...] = jnp.zeros_like(dk_acc)
        dv_acc[...] = jnp.zeros_like(dv_acc)

    clear()

    @pl.loop(0, heads)
    def _(head):
        dq_acc[head] = compute(0, head)

    own = [(dk_acc[...] * scale).T.astype(jnp.bfloat16), dv_acc[...].T.astype(jnp.bfloat16)]
    for kind in range(2):
        if group == 1:
            dkv_out[kind, :, my_cols] = own[kind]
        else:
            dkv_land[ctx % group, kind, :, my_cols] = own[kind]

    def arrive(step):
        kv_arrival(step, 0).wait_recv()
        kv_arrival(step, 1).wait_recv()
        clear()

    def give_back(step):
        dkv_send[step, 0] = (dk_acc[...] * scale).T.astype(jnp.bfloat16)
        d_copy(step, 0).start()
        dkv_send[step, 1] = dv_acc[...].T.astype(jnp.bfloat16)
        d_copy(step, 1).start()

    @pl.loop(1, n_ctx - 1)
    def _(step):
        arrive(step)

        @pl.loop(0, heads)
        def _(head):
            dq_acc[head] = compute(step, head)

        give_back(step)

    last = n_ctx - 1
    arrive(last)

    @pl.loop(0, heads)
    def _(head):
        total = compute(last, head) * scale
        dq_acc[head] = total
        dq_send[head] = total.astype(jnp.bfloat16)

        @pl.loop(1, n_rep)
        def _(step):
            q_copy(step, head).start()

    give_back(last)

    @pl.loop(1, n_ctx)
    def _(step):
        for kind in range(2):
            kv_copy(step, kind).wait_send()

    at = pl.ds(pl.multiple_of(rep * rows, rows), rows)

    @pl.loop(0, heads)
    def _(head):
        @pl.loop(1, n_rep)
        def _(step):
            q_copy(step, head).wait_recv()

        total = dq_acc[head, at, :]
        for step in range(1, n_rep):
            total = total + dq_land[step, head].astype(jnp.float32)
        dq_out[:, head_cols(head)] = total.astype(jnp.bfloat16)

    @pl.loop(1, n_ctx)
    def _(step):
        for kind in range(2):
            d_copy(step, kind).wait_send()
            d_arrival(step, kind).wait_recv()

    @pl.loop(0, heads)
    def _(head):
        @pl.loop(1, n_rep)
        def _(step):
            q_copy(step, head).wait_send()

    if group > 1:
        for kind in range(2):
            parts = [dkv_land[j, kind] for j in range(group)]
            while len(parts) > 1:
                parts = [
                    (parts[i].astype(jnp.float32) + parts[i + 1].astype(jnp.float32)).astype(jnp.bfloat16)
                    for i in range(0, len(parts), 2)
                ]
            dkv_out[kind] = parts[0]


def on_device(queries, keys, values, forward_output, output_gradient, log_sum_norm, block_attend_mask):
    n_ctx = lax.axis_size("ctx")
    n_rep = lax.axis_size("rep")
    group = n_ctx // KEY_VALUE_HEADS
    n_q, width = queries.shape
    heads = width // HEAD_SIZE
    rows = n_q // n_rep
    share = keys.shape[0]
    assert share == BLK
    any_spec = pl.BlockSpec(memory_space=pl.ANY)
    vmem = pl.BlockSpec(memory_space=pltpu.VMEM)
    smem = pl.BlockSpec(memory_space=pltpu.SMEM)
    bf16, f32 = jnp.bfloat16, jnp.float32
    land_group = group if group > 1 else 1
    land_cols = keys.shape[1] if group > 1 else HEAD_SIZE
    dq, dkv = pl.pallas_call(
        functools.partial(kernel, n_ctx, n_rep, heads, group),
        out_shape=(
            jax.ShapeDtypeStruct((rows, width), bf16),
            jax.ShapeDtypeStruct((2, share, keys.shape[1]), bf16),
        ),
        in_specs=[any_spec] * 5 + [vmem, smem],
        out_specs=(vmem, vmem),
        scratch_shapes=[
            pltpu.VMEM((n_q, width), bf16),
            pltpu.VMEM((n_q, width), bf16),
            pltpu.VMEM((n_q, width), bf16),
            pltpu.VMEM((heads, HEAD_SIZE, n_q), bf16),
            pltpu.VMEM((heads, HEAD_SIZE, n_q), bf16),
            pltpu.VMEM((heads, n_q, BLK), f32),
            pltpu.VMEM((heads, n_q, BLK), f32),
            pltpu.VMEM((n_ctx, 2, BLK, HEAD_SIZE), bf16),
            pltpu.VMEM((HEAD_SIZE, BLK), f32),
            pltpu.VMEM((HEAD_SIZE, BLK), f32),
            pltpu.VMEM((heads, n_q, HEAD_SIZE), f32),
            pltpu.VMEM((n_ctx, 2, BLK, HEAD_SIZE), bf16),
            pltpu.VMEM((heads, n_q, HEAD_SIZE), bf16),
            pltpu.VMEM((n_rep, heads, rows, HEAD_SIZE), bf16),
            pltpu.VMEM((land_group, 2, BLK, land_cols), bf16),
            pltpu.SemaphoreType.DMA((5,)),
            pltpu.SemaphoreType.DMA((n_ctx, 2)),
            pltpu.SemaphoreType.DMA((n_ctx, 2)),
            pltpu.SemaphoreType.DMA((n_ctx, 2)),
            pltpu.SemaphoreType.DMA((n_ctx, 2)),
            pltpu.SemaphoreType.DMA((n_rep, heads)),
            pltpu.SemaphoreType.DMA((n_rep, heads)),
        ],
        compiler_params=pltpu.CompilerParams(
            collective_id=0, has_side_effects=True, vmem_limit_bytes=48 * 1024 * 1024
        ),
    )(keys, values, queries, forward_output, output_gradient, log_sum_norm, block_attend_mask)
    return dq, dkv[0], dkv[1]


def solution(mesh):
    in_specs = (
        P(None, "ctx"),
        P(("ctx", "rep"), None),
        P(("ctx", "rep"), None),
        P(None, "ctx"),
        P(None, "ctx"),
        P("ctx", None),
        P("ctx", None, None),
    )
    out_specs = (P("rep", "ctx"), P(("ctx", "rep"), None), P(("ctx", "rep"), None))
    return jax.shard_map(
        on_device, mesh=mesh, in_specs=in_specs, out_specs=out_specs, check_vma=False
    )
```

time: 168 us -> 64.3 us (0.38)
  Pallas kernels: 0 us -> 54.7 us
  local copies, waits for them, and re-layouts: 57.1 us -> 8.52 us
  matrix products: 28.1 us -> 0 us
  waiting for transfers between devices: 21.3 us -> 0 us
  blocking collectives: 20.1 us -> 0 us
  between operations: 14.8 us -> 0.66 us
  other arithmetic: 14.1 us -> 0 us
  starting transfers between devices: 10.4 us -> 0 us
    pallas_call x0 -> x1, Pallas kernels: none -> 54.7 us  [on_device(): pl.pallas_call(functools.partial(kernel, n_ctx, n_rep, heads, group), out...]
    dot_general x10 -> x0, matrix products: 28.1 us -> none  [the longest x2 10.5 us: one_turn(): jnp.einsum('hqd,kd->hqk', query_heads, key_tile, preferred_element_type=j...]
    reshape x2 -> x0, local copies, waits for them, and re-layouts: 20.6 us -> none  [one_turn(): mask_full = jnp.broadcast_to(mask_tile[:, :, None, :, None].astype(jnp.fl...]
    all_to_all x1 -> x0, blocking collectives: 20.1 us -> none  [on_device(): lax.all_to_all(grad_parts, 'ctx', split_axis=1, concat_axis=1, tiled=True)]
    reduce_scatter x1 -> x0, waiting for transfers between devices: 14.3 us -> none  [on_device(): lax.psum_scatter(query_terms, 'rep', scatter_dimension=0, tiled=True)]
    all_to_all x2 -> x0, starting transfers between devices: 10.4 us -> none  [the longest x1 6.33 us: on_device(): lax.all_to_all(spread(keys), 'ctx', split_axis=1, concat_axis=0, tiled=True)]
    broadcast_in_dim x3 -> x0, local copies, waits for them, and re-layouts: 10.3 us -> none  [the longest x2 8.75 us: one_turn(): jnp.broadcast_to(mask_tile[:, :, None, :, None].astype(jnp.float32), (hea...]
    while x18 -> x0, local copies, waits for them, and re-layouts: 8.72 us -> none
  transfers between devices with their start and end apart: 3 -> 0, of which waited for: 2 -> 0; matrix products, arithmetic and copies ran while one was open for 9% -> 0% of each run, Pallas kernels for 0% -> 0%
where the time goes in v1:
time: 64.3 us; the launch traced here: 63.9 us
  Pallas kernels  54.7 us (85%)
  local copies, waits for them, and re-layouts  8.52 us (13%)
  between operations  0.66 us (1%)
    pallas_call x1, Pallas kernels, on_device(): pl.pallas_call(functools.partial(kernel, n_ctx, n_rep, heads, group), out...  54.7 us
    unnamed x15, local copies, waits for them, and re-layouts  7.7 us

profile of v1, /device:TPU:0, one launch (start us, length us, event | category | flops | bytes accessed | tf_op | source)
XLA Modules:
  0.0 63.9 jit_solution(5036259956868449331)
XLA Ops:
  0.6 0.0 copy-start
  0.6 1.2 %copy-done = bf16[512,1024]{1,0:T(8,128)(2,1)S(1)} copy-done((bf16[512,1024]{1,0:T(8,128)(2,1)S(1)}, bf16[512,1024]{1,0:T(8,128)(2,1)}, u32[]{:S(2)}) %copy-start) | copy-done | bytes 1048600
  1.9 0.0 copy-start.1
  1.9 1.2 %copy-done.1 = bf16[512,1024]{1,0:T(8,128)(2,1)S(1)} copy-done((bf16[512,1024]{1,0:T(8,128)(2,1)S(1)}, bf16[512,1024]{1,0:T(8,128)(2,1)}, u32[]{:S(2)}) %copy-start.1) | copy-done | bytes 1048600
  3.1 0.0 copy-start.2
  3.1 1.2 %copy-done.2 = bf16[512,1024]{1,0:T(8,128)(2,1)S(1)} copy-done((bf16[512,1024]{1,0:T(8,128)(2,1)S(1)}, bf16[512,1024]{1,0:T(8,128)(2,1)}, u32[]{:S(2)}) %copy-start.2) | copy-done | bytes 1048600
  4.3 0.0 copy-start.3
  4.3 0.9 %copy-done.3 = bf16[128,1024]{1,0:T(8,128)(2,1)S(1)} copy-done((bf16[128,1024]{1,0:T(8,128)(2,1)S(1)}, bf16[128,1024]{1,0:T(8,128)(2,1)}, u32[]{:S(2)}) %copy-start.3) | copy-done | bytes 262168
  5.3 0.0 copy-start.4
  5.3 0.9 %copy-done.4 = bf16[128,1024]{1,0:T(8,128)(2,1)S(1)} copy-done((bf16[128,1024]{1,0:T(8,128)(2,1)S(1)}, bf16[128,1024]{1,0:T(8,128)(2,1)}, u32[]{:S(2)}) %copy-start.4) | copy-done | bytes 262168
  6.2 0.0 copy-start.5
  6.2 0.7 %copy-done.5 = f32[8,512]{1,0:T(8,128)S(1)} copy-done((f32[8,512]{1,0:T(8,128)S(1)}, f32[8,512]{1,0:T(8,128)}, u32[]{:S(2)}) %copy-start.5) | copy-done | bytes 16408
  6.9 0.0 copy-start.6
  6.9 0.7 %copy-done.6 = s32[8,4,32]{2,1,0:T(4,128)S(1)} copy-done((s32[8,4,32]{2,1,0:T(4,128)S(1)}, s32[8,4,32]{2,1,0:T(4,128)}, u32[]{:S(2)}) %copy-start.6) | copy-done | bytes 4120
  7.6 54.7 %shard_map.94 = (bf16[128,1024]{1,0:T(8,128)(2,1)S(1)}, bf16[2,128,1024]{2,1,0:T(8,128)(2,1)S(1)}) custom-call(bf16[128,1024]{1,0:T(8,128)(2,1)S(1)} %copy-done.3, bf16[128,1024]{1,0:T(8,128)(2,1)S(1)} %copy-done.4, bf16[512,1024]{1,0:T(8,128)(2,1)S(1)} %copy-done, bf16[512,1024]{1,0:T(8,128)(2,1)S(1)} %copy-done.1, bf16[512,1024]{1,0:T(8,128)(2,1)S(1)} %copy-done.2, ...), custom_call_target="tpu_custom_call" | custom-call | tf_op jit(solution)/shard_map/pallas_call | solution.py:316
  62.4 0.8 %slice_bitcast_fusion = (bf16[128,1024]{1,0:T(8,128)(2,1)}, bf16[128,1024]{1,0:T(8,128)(2,1)}) fusion(bf16[2,128,1024]{2,1,0:T(8,128)(2,1)S(1)} %get-tuple-element.6), kind=kLoop, calls=%fused_computation | loop fusion | bytes 1048576 | tf_op jit(solution)/shard_map/squeeze | solution.py:352
  63.2 0.7 %copy.11 = bf16[128,1024]{1,0:T(8,128)(2,1)} copy(bf16[128,1024]{1,0:T(8,128)(2,1)S(1)} %get-tuple-element.12) | data formatting | bytes 524288
Async XLA Ops:
  0.6 1.2 %copy-start = (bf16[512,1024]{1,0:T(8,128)(2,1)S(1)}, bf16[512,1024]{1,0:T(8,128)(2,1)}, u32[]{:S(2)}) copy-start(bf16[512,1024]{1,0:T(8,128)(2,1)} %queries.1) | copy-start | bytes 3145732
  1.9 1.2 %copy-start.1 = (bf16[512,1024]{1,0:T(8,128)(2,1)S(1)}, bf16[512,1024]{1,0:T(8,128)(2,1)}, u32[]{:S(2)}) copy-start(bf16[512,1024]{1,0:T(8,128)(2,1)} %fwd_out.1) | copy-start | bytes 3145732
  3.1 1.2 %copy-start.2 = (bf16[512,1024]{1,0:T(8,128)(2,1)S(1)}, bf16[512,1024]{1,0:T(8,128)(2,1)}, u32[]{:S(2)}) copy-start(bf16[512,1024]{1,0:T(8,128)(2,1)} %grad_out.1) | copy-start | bytes 3145732
  4.3 0.9 %copy-start.3 = (bf16[128,1024]{1,0:T(8,128)(2,1)S(1)}, bf16[128,1024]{1,0:T(8,128)(2,1)}, u32[]{:S(2)}) copy-start(bf16[128,1024]{1,0:T(8,128)(2,1)} %keys.1) | copy-start | bytes 786436
  5.3 0.9 %copy-start.4 = (bf16[128,1024]{1,0:T(8,128)(2,1)S(1)}, bf16[128,1024]{1,0:T(8,128)(2,1)}, u32[]{:S(2)}) copy-start(bf16[128,1024]{1,0:T(8,128)(2,1)} %values.1) | copy-start | bytes 786436
  6.2 0.7 %copy-start.5 = (f32[8,512]{1,0:T(8,128)S(1)}, f32[8,512]{1,0:T(8,128)}, u32[]{:S(2)}) copy-start(f32[8,512]{1,0:T(8,128)} %norm.1) | copy-start | bytes 49156
  6.9 0.7 %copy-start.6 = (s32[8,4,32]{2,1,0:T(4,128)S(1)}, s32[8,4,32]{2,1,0:T(4,128)}, u32[]{:S(2)}) copy-start(s32[8,4,32]{2,1,0:T(4,128)} %mask.1) | copy-start | bytes 12292

commit v2 on v1

--- a/solution.py
+++ b/solution.py
@@ -13,6 +13,8 @@
 MESH = pl.DeviceIdType.MESH
 LOG2_E = 1.4426950408889634
 MASKED = 1e30
+UN = 4
+PAIR = 2 * BLK
 
 
 def partner_of(index, step, count):
@@ -34,8 +36,8 @@
     queries,
     fwd_out,
     grad_out,
-    norm,
-    mask,
+    norm_in,
+    mask_in,
     dq_out,
     dkv_out,
     q_v,
@@ -53,6 +55,8 @@
     dq_send,
     dq_land,
     dkv_land,
+    norm,
+    mask,
     load_sem,
     kv_send_sem,
     kv_recv_sem,
@@ -70,15 +74,23 @@
     def head_cols(head):
         return pl.ds(pl.multiple_of(head * HEAD_SIZE, HEAD_SIZE), HEAD_SIZE)
 
+    def half(index):
+        return pl.ds(pl.multiple_of((index % 2) * BLK, BLK), BLK)
+
+    def kv_place(source, kind):
+        return kv_v.at[source // 2, kind, half(source)]
+
     my_head = ctx // group
     my_cols = head_cols(my_head)
 
     loads = [
-        pltpu.make_async_copy(keys.at[:, my_cols], kv_v.at[ctx, 0], load_sem.at[0]),
-        pltpu.make_async_copy(values.at[:, my_cols], kv_v.at[ctx, 1], load_sem.at[1]),
+        pltpu.make_async_copy(keys.at[:, my_cols], kv_place(ctx, 0), load_sem.at[0]),
+        pltpu.make_async_copy(values.at[:, my_cols], kv_place(ctx, 1), load_sem.at[1]),
         pltpu.make_async_copy(grad_out, g_v, load_sem.at[2]),
         pltpu.make_async_copy(fwd_out, o_v, load_sem.at[3]),
         pltpu.make_async_copy(queries, q_v, load_sem.at[4]),
+        pltpu.make_async_copy(norm_in, norm, load_sem.at[5]),
+        pltpu.make_async_copy(mask_in, mask, load_sem.at[6]),
     ]
     for load in loads:
         load.start()
@@ -102,7 +114,7 @@
         source = (keys, values)[kind]
         return pltpu.make_async_remote_copy(
             src_ref=source.at[:, head_cols(peer // group)],
-            dst_ref=kv_v.at[ctx, kind],
+            dst_ref=kv_place(ctx, kind),
             send_sem=kv_send_sem.at[step, kind],
             recv_sem=kv_recv_sem.at[step, kind],
             device_id=(peer, rep),
@@ -113,7 +125,7 @@
         peer = partner_of(ctx, step, n_ctx)
         return pltpu.make_async_remote_copy(
             src_ref=(keys, values)[kind].at[:, my_cols],
-            dst_ref=kv_v.at[peer, kind],
+            dst_ref=kv_place(peer, kind),
             send_sem=kv_send_sem.at[step, kind],
             recv_sem=kv_recv_sem.at[step, kind],
             device_id=(peer, rep),
@@ -150,7 +162,7 @@
     def d_copy(step, kind):
         peer = partner_of(ctx, step, n_ctx)
         return pltpu.make_async_remote_copy(
-            src_ref=dkv_send.at[step, kind],
+            src_ref=dkv_send.at[step // 2, kind, half(peer)],
             dst_ref=landing(ctx, kind),
             send_sem=d_send_sem.at[step, kind],
             recv_sem=d_recv_sem.at[step, kind],
@@ -161,7 +173,7 @@
     def d_arrival(step, kind):
         peer = partner_of(ctx, step, n_ctx)
         return pltpu.make_async_remote_copy(
-            src_ref=dkv_send.at[step, kind],
+            src_ref=dkv_send.at[step // 2, kind, half(peer)],
             dst_ref=landing(peer, kind),
             send_sem=d_send_sem.at[step, kind],
             recv_sem=d_recv_sem.at[step, kind],
@@ -181,25 +193,31 @@
             device_id_type=MESH,
         )
 
-    def compute(step, head):
-        source = partner_of(ctx, step, n_ctx)
+    def compute(turn, head):
+        chip = partner_of(ctx // 2, turn, n_ctx // 2)
         cols = head_cols(head)
-        k = kv_v[source, 0]
-        v = kv_v[source, 1]
+        k = kv_v[chip, 0]
+        v = kv_v[chip, 1]
         q = q_v[:, cols]
         g = g_v[:, cols]
         nt = (((1,), (1,)), ((), ()))
         s = lax.dot_general(q, k, nt, preferred_element_type=jnp.float32)
         gw = lax.dot_general(g, v, nt, preferred_element_type=jnp.float32)
-        key_block = source * n_rep + rep
-        parts = []
+        p_rows, ds_rows = [], []
         for qb in range(n_q // BLK):
-            off = (1 - mask[head, qb, key_block]).astype(jnp.float32) * MASKED
             span = slice(qb * BLK, (qb + 1) * BLK)
-            parts.append(jnp.exp2(s[span] * (scale * LOG2_E) - (norm_b[head, span, :] + off)))
-        w = jnp.concatenate(parts, axis=0)
-        p = w.astype(jnp.bfloat16)
-        ds = (w * (gw - dots_b[head])).astype(jnp.bfloat16)
+            p_cols, ds_cols = [], []
+            for j in range(2):
+                part = slice(j * BLK, (j + 1) * BLK)
+                key_block = (2 * chip + j) * n_rep + rep
+                off = (1 - mask[head, qb, key_block]).astype(jnp.float32) * MASKED
+                w = jnp.exp2(s[span, part] * (scale * LOG2_E) - (norm_b[head, span, :] + off))
+                p_cols.append(w.astype(jnp.bfloat16))
+                ds_cols.append((w * (gw[span, part] - dots_b[head, span, :])).astype(jnp.bfloat16))
+            p_rows.append(jnp.concatenate(p_cols, axis=1))
+            ds_rows.append(jnp.concatenate(ds_cols, axis=1))
+        p = jnp.concatenate(p_rows, axis=0)
+        ds = jnp.concatenate(ds_rows, axis=0)
         dk_acc[...] += jnp.dot(qt_v[head], ds, preferred_element_type=jnp.float32)
         dv_acc[...] += jnp.dot(gt_v[head], p, preferred_element_type=jnp.float32)
         return dq_acc[head] + jnp.dot(ds, k, preferred_element_type=jnp.float32)
@@ -208,44 +226,54 @@
         dk_acc[...] = jnp.zeros_like(dk_acc)
         dv_acc[...] = jnp.zeros_like(dv_acc)
 
+    def arrive(step):
+        for kind in range(2):
+            kv_arrival(step, kind).wait_recv()
+
+    def give_back(turn):
+        dkv_send[turn, 0] = (dk_acc[...] * scale).T.astype(jnp.bfloat16)
+        dkv_send[turn, 1] = dv_acc[...].T.astype(jnp.bfloat16)
+
+    def send_back(step):
+        for kind in range(2):
+            d_copy(step, kind).start()
+
+    arrive(1)
     clear()
 
-    @pl.loop(0, heads)
+    @pl.loop(0, heads, unroll=UN)
     def _(head):
         dq_acc[head] = compute(0, head)
 
-    own = [(dk_acc[...] * scale).T.astype(jnp.bfloat16), dv_acc[...].T.astype(jnp.bfloat16)]
+    give_back(0)
+    send_back(1)
     for kind in range(2):
+        own = dkv_send[0, kind, half(ctx), :]
         if group == 1:
-            dkv_out[kind, :, my_cols] = own[kind]
+            dkv_out[kind, :, my_cols] = own
         else:
-            dkv_land[ctx % group, kind, :, my_cols] = own[kind]
-
-    def arrive(step):
-        kv_arrival(step, 0).wait_recv()
-        kv_arrival(step, 1).wait_recv()
+            dkv_land[ctx % group, kind, :, my_cols] = own
+
+    @pl.loop(1, n_ctx // 2 - 1)
+    def _(turn):
+        arrive(2 * turn)
+        arrive(2 * turn + 1)
         clear()
 
-    def give_back(step):
-        dkv_send[step, 0] = (dk_acc[...] * scale).T.astype(jnp.bfloat16)
-        d_copy(step, 0).start()
-        dkv_send[step, 1] = dv_acc[...].T.astype(jnp.bfloat16)
-        d_copy(step, 1).start()
-
-    @pl.loop(1, n_ctx - 1)
-    def _(step):
-        arrive(step)
-
-        @pl.loop(0, heads)
+        @pl.loop(0, heads, unroll=UN)
         def _(head):
-            dq_acc[head] = compute(step, head)
-
-        give_back(step)
-
-    last = n_ctx - 1
-    arrive(last)
-
-    @pl.loop(0, heads)
+            dq_acc[head] = compute(turn, head)
+
+        give_back(turn)
+        send_back(2 * turn)
+        send_back(2 * turn + 1)
+
+    last = n_ctx // 2 - 1
+    arrive(2 * last)
+    arrive(2 * last + 1)
+    clear()
+
+    @pl.loop(0, heads, unroll=UN)
     def _(head):
         total = compute(last, head) * scale
         dq_acc[head] = total
@@ -256,6 +284,8 @@
             q_copy(step, head).start()
 
     give_back(last)
+    send_back(2 * last)
+    send_back(2 * last + 1)
 
     @pl.loop(1, n_ctx)
     def _(step):
@@ -307,9 +337,8 @@
     rows = n_q // n_rep
     share = keys.shape[0]
     assert share == BLK
-    any_spec = pl.BlockSpec(memory_space=pl.ANY)
+    hbm = pl.BlockSpec(memory_space=pltpu.HBM)
     vmem = pl.BlockSpec(memory_space=pltpu.VMEM)
-    smem = pl.BlockSpec(memory_space=pltpu.SMEM)
     bf16, f32 = jnp.bfloat16, jnp.float32
     land_group = group if group > 1 else 1
     land_cols = keys.shape[1] if group > 1 else HEAD_SIZE
@@ -319,7 +348,7 @@
             jax.ShapeDtypeStruct((rows, width), bf16),
             jax.ShapeDtypeStruct((2, share, keys.shape[1]), bf16),
         ),
-        in_specs=[any_spec] * 5 + [vmem, smem],
+        in_specs=[hbm] * 7,
         out_specs=(vmem, vmem),
         scratch_shapes=[
             pltpu.VMEM((n_q, width), bf16),
@@ -329,15 +358,17 @@
             pltpu.VMEM((heads, HEAD_SIZE, n_q), bf16),
             pltpu.VMEM((heads, n_q, BLK), f32),
             pltpu.VMEM((heads, n_q, BLK), f32),
-            pltpu.VMEM((n_ctx, 2, BLK, HEAD_SIZE), bf16),
-            pltpu.VMEM((HEAD_SIZE, BLK), f32),
-            pltpu.VMEM((HEAD_SIZE, BLK), f32),
+            pltpu.VMEM((n_ctx // 2, 2, PAIR, HEAD_SIZE), bf16),
+            pltpu.VMEM((HEAD_SIZE, PAIR), f32),
+            pltpu.VMEM((HEAD_SIZE, PAIR), f32),
             pltpu.VMEM((heads, n_q, HEAD_SIZE), f32),
-            pltpu.VMEM((n_ctx, 2, BLK, HEAD_SIZE), bf16),
+            pltpu.VMEM((n_ctx // 2, 2, PAIR, HEAD_SIZE), bf16),
             pltpu.VMEM((heads, n_q, HEAD_SIZE), bf16),
             pltpu.VMEM((n_rep, heads, rows, HEAD_SIZE), bf16),
             pltpu.VMEM((land_group, 2, BLK, land_cols), bf16),
-            pltpu.SemaphoreType.DMA((5,)),
+            pltpu.VMEM(log_sum_norm.shape, f32),
+            pltpu.SMEM(block_attend_mask.shape, jnp.int32),
+            pltpu.SemaphoreType.DMA((7,)),
             pltpu.SemaphoreType.DMA((n_ctx, 2)),
             pltpu.SemaphoreType.DMA((n_ctx, 2)),
             pltpu.SemaphoreType.DMA((n_ctx, 2)),

time: 64.3 us -> 46.4 us (0.72)
  Pallas kernels: 54.7 us -> 36.8 us
    pallas_call x1, Pallas kernels: 54.7 us -> 36.8 us  [on_device(): pl.pallas_call(functools.partial(kernel, n_ctx, n_rep, heads, group), out...]
where the time goes in v2:
time: 46.4 us; the launch traced here: 46 us
  Pallas kernels  36.8 us (79%)
  local copies, waits for them, and re-layouts  8.52 us (18%)
  between operations  0.66 us (1%)
    pallas_call x1, Pallas kernels, on_device(): pl.pallas_call(functools.partial(kernel, n_ctx, n_rep, heads, group), out...  36.8 us
    unnamed x15, local copies, waits for them, and re-layouts  7.7 us

profile of v2, /device:TPU:0, one launch (start us, length us, event | category | flops | bytes accessed | tf_op | source)
XLA Modules:
  0.0 46.0 jit_solution(18412598574926513657)
XLA Ops:
  0.6 0.0 copy-start
  0.6 1.2 %copy-done = bf16[512,1024]{1,0:T(8,128)(2,1)S(1)} copy-done((bf16[512,1024]{1,0:T(8,128)(2,1)S(1)}, bf16[512,1024]{1,0:T(8,128)(2,1)}, u32[]{:S(2)}) %copy-start) | copy-done | bytes 1048600
  1.9 0.0 copy-start.1
  1.9 1.2 %copy-done.1 = bf16[512,1024]{1,0:T(8,128)(2,1)S(1)} copy-done((bf16[512,1024]{1,0:T(8,128)(2,1)S(1)}, bf16[512,1024]{1,0:T(8,128)(2,1)}, u32[]{:S(2)}) %copy-start.1) | copy-done | bytes 1048600
  3.1 0.0 copy-start.2
  3.1 1.2 %copy-done.2 = bf16[512,1024]{1,0:T(8,128)(2,1)S(1)} copy-done((bf16[512,1024]{1,0:T(8,128)(2,1)S(1)}, bf16[512,1024]{1,0:T(8,128)(2,1)}, u32[]{:S(2)}) %copy-start.2) | copy-done | bytes 1048600
  4.3 0.0 copy-start.3
  4.3 0.9 %copy-done.3 = bf16[128,1024]{1,0:T(8,128)(2,1)S(1)} copy-done((bf16[128,1024]{1,0:T(8,128)(2,1)S(1)}, bf16[128,1024]{1,0:T(8,128)(2,1)}, u32[]{:S(2)}) %copy-start.3) | copy-done | bytes 262168
  5.3 0.0 copy-start.4
  5.3 0.9 %copy-done.4 = bf16[128,1024]{1,0:T(8,128)(2,1)S(1)} copy-done((bf16[128,1024]{1,0:T(8,128)(2,1)S(1)}, bf16[128,1024]{1,0:T(8,128)(2,1)}, u32[]{:S(2)}) %copy-start.4) | copy-done | bytes 262168
  6.2 0.0 copy-start.5
  6.2 0.7 %copy-done.5 = f32[8,512]{1,0:T(8,128)S(1)} copy-done((f32[8,512]{1,0:T(8,128)S(1)}, f32[8,512]{1,0:T(8,128)}, u32[]{:S(2)}) %copy-start.5) | copy-done | bytes 16408
  6.9 0.0 copy-start.6
  6.9 0.7 %copy-done.6 = s32[8,4,32]{2,1,0:T(4,128)S(1)} copy-done((s32[8,4,32]{2,1,0:T(4,128)S(1)}, s32[8,4,32]{2,1,0:T(4,128)}, u32[]{:S(2)}) %copy-start.6) | copy-done | bytes 4120
  7.6 36.8 %shard_map.94 = (bf16[128,1024]{1,0:T(8,128)(2,1)S(1)}, bf16[2,128,1024]{2,1,0:T(8,128)(2,1)S(1)}) custom-call(bf16[128,1024]{1,0:T(8,128)(2,1)S(1)} %copy-done.3, bf16[128,1024]{1,0:T(8,128)(2,1)S(1)} %copy-done.4, bf16[512,1024]{1,0:T(8,128)(2,1)S(1)} %copy-done, bf16[512,1024]{1,0:T(8,128)(2,1)S(1)} %copy-done.1, bf16[512,1024]{1,0:T(8,128)(2,1)S(1)} %copy-done.2, ...), custom_call_target="tpu_custom_call" | custom-call | tf_op jit(solution)/shard_map/pallas_call | solution.py:345
  44.5 0.8 %slice_bitcast_fusion = (bf16[128,1024]{1,0:T(8,128)(2,1)}, bf16[128,1024]{1,0:T(8,128)(2,1)}) fusion(bf16[2,128,1024]{2,1,0:T(8,128)(2,1)S(1)} %get-tuple-element.6), kind=kLoop, calls=%fused_computation | loop fusion | bytes 1048576 | tf_op jit(solution)/shard_map/squeeze | solution.py:383
  45.3 0.7 %copy.11 = bf16[128,1024]{1,0:T(8,128)(2,1)} copy(bf16[128,1024]{1,0:T(8,128)(2,1)S(1)} %get-tuple-element.12) | data formatting | bytes 524288
Async XLA Ops:
  0.6 1.2 %copy-start = (bf16[512,1024]{1,0:T(8,128)(2,1)S(1)}, bf16[512,1024]{1,0:T(8,128)(2,1)}, u32[]{:S(2)}) copy-start(bf16[512,1024]{1,0:T(8,128)(2,1)} %queries.1) | copy-start | bytes 3145732
  1.9 1.2 %copy-start.1 = (bf16[512,1024]{1,0:T(8,128)(2,1)S(1)}, bf16[512,1024]{1,0:T(8,128)(2,1)}, u32[]{:S(2)}) copy-start(bf16[512,1024]{1,0:T(8,128)(2,1)} %fwd_out.1) | copy-start | bytes 3145732
  3.1 1.2 %copy-start.2 = (bf16[512,1024]{1,0:T(8,128)(2,1)S(1)}, bf16[512,1024]{1,0:T(8,128)(2,1)}, u32[]{:S(2)}) copy-start(bf16[512,1024]{1,0:T(8,128)(2,1)} %grad_out.1) | copy-start | bytes 3145732
  4.3 0.9 %copy-start.3 = (bf16[128,1024]{1,0:T(8,128)(2,1)S(1)}, bf16[128,1024]{1,0:T(8,128)(2,1)}, u32[]{:S(2)}) copy-start(bf16[128,1024]{1,0:T(8,128)(2,1)} %keys.1) | copy-start | bytes 786436
  5.3 0.9 %copy-start.4 = (bf16[128,1024]{1,0:T(8,128)(2,1)S(1)}, bf16[128,1024]{1,0:T(8,128)(2,1)}, u32[]{:S(2)}) copy-start(bf16[128,1024]{1,0:T(8,128)(2,1)} %values.1) | copy-start | bytes 786436
  6.2 0.7 %copy-start.5 = (f32[8,512]{1,0:T(8,128)S(1)}, f32[8,512]{1,0:T(8,128)}, u32[]{:S(2)}) copy-start(f32[8,512]{1,0:T(8,128)} %norm_in.1) | copy-start | bytes 49156
  6.9 0.7 %copy-start.6 = (s32[8,4,32]{2,1,0:T(4,128)S(1)}, s32[8,4,32]{2,1,0:T(4,128)}, u32[]{:S(2)}) copy-start(s32[8,4,32]{2,1,0:T(4,128)} %mask_in.1) | copy-start | bytes 12292
